TPU v7x, 256 devices: a whole 4x4x8 slice. The times are simulated.
256 devices in a mesh: wide: 16 (over x, y_lo, core), narrow: 16 (over z, y_hi).
Axes of the slice: x: 4, y: 4 (y_hi: 2, y_lo: 2; y = y_hi * 2 + y_lo), z: 8, core: 2. Of those that a mesh axis runs over, the one named last changes fastest.
Arguments:
- hamiltonian_tiles: float32 [24576, 24576], P('wide', 'narrow'), may hold values from -0.02734375 to 0.02734375
- row_columns: int32 [16, 16], P('wide'), may hold values from 0 to 15, as said below
- start_vectors: float32 [24576, 128], P(('wide', 'narrow')), may hold values from -60 to 60
Outputs:
- new_vectors: float32 [24576, 128], P(('wide', 'narrow'))
Inputs may be any that keep to these rules, and one draw needn't show every extreme that they name: For block row r = w + j // 16, row_columns[w, j] = (r + d) mod 16, with d = 0 where j % 16 = 0 and, for the other tiles of that block row, distinct d between 1 and 15; a block's mirror may also be stored.
All inputs are finite; a program needn't handle non-finite values.
Results may differ from a plain program's by a relative error of at most 0.0003.
Values sent between devices are 32-bit elements; how exact they have to be, the bound alone decides.
No kernel may reach another device: no remote copies, remote signals or barrier semaphores. Data moves between devices by JAX's collectives and lax.ppermute only.
A program may use at most 64 MiB of HBM per device.

v0:
```python
import jax
import jax.numpy as jnp
from jax import lax
from jax.sharding import Mesh
from jax.sharding import PartitionSpec as P

ITERS = 2
NS_STEPS = 5
NARROW = ("narrow_0", "narrow_1")
WIDE = ("wide_0", "wide_1", "wide_2")
WIDE_NARROW = ("wide_0", "wide_1", "wide_2", "narrow_0", "narrow_1")


def laid_out(parts, dim):
    parts = jnp.moveaxis(parts, 0, dim)
    dims = parts.shape
    return parts.reshape(*dims[:dim], dims[dim] * dims[dim + 1], *dims[dim + 2 :])


def from_everyone(value, axis):
    size = lax.axis_size(axis)
    return lax.all_to_all(
        jnp.broadcast_to(value[None], (size, *value.shape)), axis, 0, 0, tiled=True
    )


def gathered_copies(value, axis, dim):
    return laid_out(from_everyone(value, axis), dim)


def side_by_side(arrays, axis, split_dim, concat_dim, along):
    widths = [a.shape[along] for a in arrays]
    both = jnp.concatenate(arrays, axis=along)
    whole = lax.all_to_all(both, axis, split_axis=split_dim, concat_axis=concat_dim, tiled=True)
    return tuple(jnp.split(whole, [sum(widths[:k]) for k in range(1, len(widths))], axis=along))


def cut_along(value, dim, size):
    dims = value.shape
    parts = value.reshape(*dims[:dim], size, dims[dim] // size, *dims[dim + 1 :])
    return jnp.moveaxis(parts, dim, 0)


def sum_at_owner(value, axis, dim):
    parts = cut_along(value, dim, lax.axis_size(axis))
    arrived = lax.all_to_all(parts, axis, split_axis=0, concat_axis=0, tiled=True)
    return arrived.sum(axis=0)


def one_axis_at_a_time(value, axes):
    for axis in axes:
        value = lax.psum(value, axis)
    return value


def orthonormalize(product, gram, total_rows):
    width = gram.shape[0]
    identity = jnp.eye(width, dtype=jnp.float32)
    scale = jnp.sqrt(jnp.sum(gram * gram) + 1e-06)
    current = gram / scale
    inverse = identity
    for repeat in range(NS_STEPS):
        middle = 1.5 * identity - 0.5 * jnp.dot(inverse, current, precision=lax.Precision.HIGHEST)
        current = jnp.dot(current, middle, precision=lax.Precision.HIGHEST)
        inverse = jnp.dot(middle, inverse, precision=lax.Precision.HIGHEST)
    return jnp.dot(product, inverse, precision=lax.Precision.HIGHEST) * jnp.sqrt(total_rows / scale)


def on_device(hamiltonian_tiles, row_columns, start_vectors):
    narrow_count = lax.axis_size(NARROW)
    wide_count = lax.axis_size(WIDE)
    my_index = lax.axis_index(NARROW)
    order_tile = hamiltonian_tiles.shape[0]
    slice_rows = start_vectors.shape[0]
    width = start_vectors.shape[1]
    per_row = order_tile // slice_rows
    rows_group = narrow_count // per_row
    my_block = my_index // per_row
    columns_row = row_columns[0]
    column_group = columns_row // rows_group
    column_place = columns_row % rows_group
    my_column_place = column_place[my_index]
    sender_block = jnp.arange(narrow_count, dtype=jnp.int32) // per_row
    back_weight = (
        (column_group[:, None] == jnp.arange(wide_count, dtype=jnp.int32)[None, :])
        & (column_place[:, None] == my_block)
    ).astype(jnp.float32)
    own_weight = (sender_block == my_block).astype(jnp.float32)
    total_rows = float(wide_count * rows_group * order_tile)
    vectors = start_vectors
    for repeat in range(ITERS):
        slices = gathered_copies(vectors, WIDE, 0)
        picked = jnp.take(slices.reshape(wide_count, slice_rows, width), column_group, axis=0)
        copies = jnp.broadcast_to(vectors[None], (narrow_count, slice_rows, width))
        got_column, got_row = side_by_side((picked, copies), NARROW, 0, 0, 1)
        row_block = lax.dynamic_index_in_dim(
            got_row.reshape(rows_group, order_tile, width), my_block, 0, keepdims=False
        )
        column_block = lax.dynamic_index_in_dim(
            got_column.reshape(rows_group, order_tile, width), my_column_place, 0, keepdims=False
        )
        direct = jnp.dot(hamiltonian_tiles, column_block, precision=lax.Precision.HIGHEST)
        transposed = lax.dot_general(
            hamiltonian_tiles, row_block, (((0,), (0,)), ((), ())), precision=lax.Precision.HIGHEST
        )
        transposed_spread = transposed.reshape(1, per_row, slice_rows, width).reshape(
            narrow_count, slice_rows, width
        )
        direct_spread = direct.reshape(1, per_row, slice_rows, width).reshape(
            narrow_count, slice_rows, width
        )
        arrived, direct_pieces = side_by_side((transposed_spread, direct_spread), NARROW, 0, 0, 1)
        direct_part = jnp.einsum(
            "n,nsk->sk", own_weight, direct_pieces, precision=lax.Precision.HIGHEST
        )
        placed = jnp.einsum("nb,nsk->bsk", back_weight, arrived, precision=lax.Precision.HIGHEST)
        moved_part = sum_at_owner(placed.reshape(wide_count * slice_rows, width), WIDE, 0)
        product = direct_part + moved_part
        local_gram = lax.dot_general(
            product, product, (((0,), (0,)), ((), ())), precision=lax.Precision.HIGHEST
        )
        gram = one_axis_at_a_time(local_gram, WIDE_NARROW)
        vectors = orthonormalize(product, gram, total_rows)
    return vectors


def solution(mesh):
    finer = Mesh(
        mesh.devices.reshape(4, 2, 2, 8, 2), ("wide_0", "wide_1", "wide_2", "narrow_0", "narrow_1")
    )
    placed = (P(WIDE, NARROW), P(WIDE, None), P(WIDE_NARROW, None))
    return jax.shard_map(
        on_device, mesh=finer, in_specs=placed, out_specs=P(WIDE_NARROW, None), check_vma=False
    )
```

profile of v0, /device:TPU:8, one launch (start us, length us, event | category | flops | bytes accessed | tf_op | source)
XLA Modules:
  0.0 773.2 jit_solution(13234159515457362002)
XLA Ops:
  6.5 1.8 broadcast_in_dim.13
  8.3 5.8 all-to-all-start
  14.1 12.1 %all-to-all-done = f32[16,96,128]{2,1,0:T(8,128)S(1)} async-done(((f32[16,96,128]{2,1,0:T(8,128)}), f32[16,96,128]{2,1,0:T(8,128)S(1)}, u32[]{:S(2)}, u32[]{:S(2)}) %all-to-all-start) | async-done | bytes 786464 | tf_op jit(solution)/shard_map/all_to_all | solution.py:22
  26.3 0.6 gather_fusion
  27.0 1.4 pad_maximum_fusion
  28.4 52.5 %all_to_all.40 = f32[16,192,128]{2,1,0:T(8,128)S(1)} all-to-all(f32[16,192,128]{2,1,0:T(8,128)S(1)} %pad_maximum_fusion), channel_id=1, replica_groups=mesh['wide_0'=4,'wide_1'=2,'wide_2'=2,'narrow_0'=8,'narrow_1'=2] {'narro..., dimensions={0} | all-to-all | bytes 3145728 | tf_op jit(solution)/shard_map/all_to_all | solution.py:34
  81.0 10.1 %convolution_bitcast_fusion.2 = f32[1536,128]{0,1:T(8,128)S(1)} fusion(f32[1536,128]{1,0:T(8,128)S(1)} %bitcast.104, f32[1536,1536]{1,0:T(8,128)S(1)} %copy-done), kind=kOutput, calls=%fused_computation.4 | convolution fusion | flops 3623878656 | bytes 11010048 | tf_op jit(solution)/shard_map/dot_general | solution.py:102
  91.2 0.3 copy.17
  91.4 7.9 %convolution_bitcast_fusion.3 = f32[1536,128]{0,1:T(8,128)S(1)} fusion(f32[1536,128]{1,0:T(8,128)S(1)} %bitcast.102, f32[1536,1536]{1,0:T(8,128)} %param.5), kind=kOutput, calls=%fused_computation.5 | convolution fusion | flops 3623878656 | bytes 11010048 | tf_op jit(solution)/shard_map/dot_general | solution.py:103
  99.4 0.3 copy.16
  99.6 1.3 pad_maximum_fusion.1
  100.9 3.9 all-to-all-start.2
  104.8 39.6 %all-to-all-done.2 = f32[16,192,128]{2,1,0:T(8,128)S(1)} async-done(((f32[16,192,128]{2,1,0:T(8,128)}), f32[16,192,128]{2,1,0:T(8,128)S(1)}, u32[]{:S(2)}, u32[]{:S(2)}) %all-to-all-start.2) | async-done | bytes 1572896 | tf_op jit(solution)/shard_map/all_to_all | solution.py:34
  144.5 0.9 fusion.12
  145.5 1.1 copy.19
  146.6 4.5 all-to-all-start.3
  151.2 0.8 fusion.16
  152.0 11.3 %all-to-all-done.3 = f32[16,96,128]{2,1,0:T(8,128)S(1)} async-done(((f32[16,96,128]{2,1,0:T(8,128)}), f32[16,96,128]{2,1,0:T(8,128)S(1)}, u32[]{:S(2)}, u32[]{:S(2)}) %all-to-all-start.3) | async-done | bytes 786464 | tf_op jit(solution)/shard_map/all_to_all | solution.py:46
  163.3 0.9 fusion.50
  164.3 40.8 %all-reduce.11.cloned.1.call-done = f32[128,128]{1,0:T(8,128)} async-done(((f32[128,128]{1,0:T(8,128)}), f32[128,128]{1,0:T(8,128)}) %all-reduce.11.cloned.1.call-update) | async-done | bytes 65552 | tf_op jit(solution)/shard_map/psum | solution.py:52
  205.2 35.0 %all-reduce.13.cloned.1.call-done = f32[128,128]{1,0:T(8,128)} async-done(((f32[128,128]{1,0:T(8,128)}), f32[128,128]{1,0:T(8,128)}) %all-reduce.13.cloned.1.call-update) | async-done | bytes 65552 | tf_op jit(solution)/shard_map/psum | solution.py:52
  240.2 32.9 %all-reduce.15.cloned.1.call-done = f32[128,128]{1,0:T(8,128)} async-done(((f32[128,128]{1,0:T(8,128)}), f32[128,128]{1,0:T(8,128)}) %all-reduce.15.cloned.1.call-update) | async-done | bytes 65552 | tf_op jit(solution)/shard_map/psum | solution.py:52
  273.2 74.9 %all-reduce.17.cloned.1.call-done = f32[128,128]{1,0:T(8,128)} async-done(((f32[128,128]{1,0:T(8,128)}), f32[128,128]{1,0:T(8,128)}) %all-reduce.17.cloned.1.call-update) | async-done | bytes 65552 | tf_op jit(solution)/shard_map/psum | solution.py:52
  348.1 34.0 %all-reduce.19.cloned.1.call-done = f32[128,128]{1,0:T(8,128)} async-done(((f32[128,128]{1,0:T(8,128)}), f32[128,128]{1,0:T(8,128)}) %all-reduce.19.cloned.1.call-update) | async-done | bytes 65552 | tf_op jit(solution)/shard_map/psum | solution.py:52
  382.1 1.5 multiply_reduce_fusion.1
  384.2 1.0 fusion.9
  385.5 1.0 fusion.20
  389.2 17.6 %all_to_all.41 = f32[16,96,128]{2,1,0:T(8,128)S(1)} all-to-all(f32[16,96,128]{2,1,0:T(8,128)S(1)} %broadcast_in_dim.14), channel_id=1, replica_groups=mesh['wide_0'=4,'wide_1'=2,'wide_2'=2,'narrow_0'=8,'narrow_1'=2] {'wide_..., dimensions={0} | all-to-all | bytes 1572864 | tf_op jit(solution)/shard_map/all_to_all | solution.py:22
  406.8 0.6 gather_fusion.1
  407.7 49.9 %all_to_all.42 = f32[16,192,128]{2,1,0:T(8,128)S(1)} all-to-all(f32[16,192,128]{2,1,0:T(8,128)S(1)} %pad_maximum_fusion.2), channel_id=1, replica_groups=mesh['wide_0'=4,'wide_1'=2,'wide_2'=2,'narrow_0'=8,'narrow_1'=2] {'narro..., dimensions={0} | all-to-all | bytes 3145728 | tf_op jit(solution)/shard_map/all_to_all | solution.py:34
  457.7 10.8 %convolution_bitcast_fusion = f32[1536,128]{0,1:T(8,128)S(1)} fusion(f32[1536,128]{1,0:T(8,128)S(1)} %bitcast.105, f32[1536,1536]{1,0:T(8,128)} %param.5), kind=kOutput, calls=%fused_computation.2 | convolution fusion | flops 3623878656 | bytes 11010048 | tf_op jit(solution)/shard_map/dot_general | solution.py:102
  468.8 7.9 %convolution_bitcast_fusion.1 = f32[1536,128]{0,1:T(8,128)S(1)} fusion(f32[1536,128]{1,0:T(8,128)S(1)} %bitcast.103, f32[1536,1536]{1,0:T(8,128)} %param.5), kind=kOutput, calls=%fused_computation.3 | convolution fusion | flops 3623878656 | bytes 11010048 | tf_op jit(solution)/shard_map/dot_general | solution.py:103
  477.1 43.7 %all_to_all.43 = f32[16,192,128]{2,1,0:T(8,128)S(1)} all-to-all(f32[16,192,128]{2,1,0:T(8,128)S(1)} %pad_maximum_fusion.3), channel_id=1, replica_groups=mesh['wide_0'=4,'wide_1'=2,'wide_2'=2,'narrow_0'=8,'narrow_1'=2] {'narro..., dimensions={0} | all-to-all | bytes 3145728 | tf_op jit(solution)/shard_map/all_to_all | solution.py:34
  520.9 0.9 fusion.10
  521.8 1.1 copy.23
  523.0 5.2 all-to-all-start.7
  528.2 0.8 fusion.14
  529.0 11.3 %all-to-all-done.7 = f32[16,96,128]{2,1,0:T(8,128)S(1)} async-done(((f32[16,96,128]{2,1,0:T(8,128)}), f32[16,96,128]{2,1,0:T(8,128)S(1)}, u32[]{:S(2)}, u32[]{:S(2)}) %all-to-all-start.7) | async-done | bytes 786464 | tf_op jit(solution)/shard_map/all_to_all | solution.py:46
  540.4 0.9 fusion.58
  541.4 40.2 %all-reduce.21.cloned.1.call-done = f32[128,128]{1,0:T(8,128)} async-done(((f32[128,128]{1,0:T(8,128)}), f32[128,128]{1,0:T(8,128)}) %all-reduce.21.cloned.1.call-update) | async-done | bytes 65552 | tf_op jit(solution)/shard_map/psum | solution.py:52
  581.7 35.0 %all-reduce.23.cloned.1.call-done = f32[128,128]{1,0:T(8,128)} async-done(((f32[128,128]{1,0:T(8,128)}), f32[128,128]{1,0:T(8,128)}) %all-reduce.23.cloned.1.call-update) | async-done | bytes 65552 | tf_op jit(solution)/shard_map/psum | solution.py:52
  616.7 32.9 %all-reduce.25.cloned.1.call-done = f32[128,128]{1,0:T(8,128)} async-done(((f32[128,128]{1,0:T(8,128)}), f32[128,128]{1,0:T(8,128)}) %all-reduce.25.cloned.1.call-update) | async-done | bytes 65552 | tf_op jit(solution)/shard_map/psum | solution.py:52
  649.6 75.0 %all-reduce.27.cloned.1.call-done = f32[128,128]{1,0:T(8,128)} async-done(((f32[128,128]{1,0:T(8,128)}), f32[128,128]{1,0:T(8,128)}) %all-reduce.27.cloned.1.call-update) | async-done | bytes 65552 | tf_op jit(solution)/shard_map/psum | solution.py:52
  724.7 34.0 %all-reduce.29.cloned.1.call-done = f32[128,128]{1,0:T(8,128)} async-done(((f32[128,128]{1,0:T(8,128)}), f32[128,128]{1,0:T(8,128)}) %all-reduce.29.cloned.1.call-update) | async-done | bytes 65552 | tf_op jit(solution)/shard_map/psum | solution.py:52
  758.7 1.5 multiply_reduce_fusion
  760.8 1.0 fusion.4
  762.1 1.0 fusion.21
  765.5 0.8 convolution_multiply_fusion.10
  (67 shorter events, 7.2 us)
Async XLA Ops:
  6.5 7.6 copy-start.1
  8.3 17.9 %all-to-all-start = ((f32[16,96,128]{2,1,0:T(8,128)}), f32[16,96,128]{2,1,0:T(8,128)S(1)}, u32[]{:S(2)}, u32[]{:S(2)}) async-start(f32[16,96,128]{2,1,0:T(8,128)} %broadcast_in_dim.13), calls=%async_computation | async-start | bytes 1572864 | tf_op jit(solution)/shard_map/all_to_all | solution.py:22
  27.0 54.1 %copy-start = (f32[1536,1536]{1,0:T(8,128)S(1)}, f32[1536,1536]{1,0:T(8,128)}, u32[]{:S(2)}) copy-start(f32[1536,1536]{1,0:T(8,128)} %param.5) | copy-start | bytes 28311556
  100.9 43.5 %all-to-all-start.2 = ((f32[16,192,128]{2,1,0:T(8,128)}), f32[16,192,128]{2,1,0:T(8,128)S(1)}, u32[]{:S(2)}, u32[]{:S(2)}) async-start(f32[16,192,128]{2,1,0:T(8,128)} %pad_maximum_fusion.1), calls=%async_computation.2 | async-start | bytes 3145728 | tf_op jit(solution)/shard_map/all_to_all | solution.py:34
  146.6 16.7 %all-to-all-start.3 = ((f32[16,96,128]{2,1,0:T(8,128)}), f32[16,96,128]{2,1,0:T(8,128)S(1)}, u32[]{:S(2)}, u32[]{:S(2)}) async-start(f32[16,96,128]{2,1,0:T(8,128)} %copy.19), calls=%async_computation.3 | async-start | bytes 1572864 | tf_op jit(solution)/shard_map/all_to_all | solution.py:46
  151.1 54.0 %all-reduce.11.cloned.1.call-start = ((), (), s32[]{:S(2)}) async-start(), calls=%async_computation.8 | async-start | bytes 131072 | tf_op jit(solution)/shard_map/psum | solution.py:52
  164.3 75.9 %all-reduce.13.cloned.1.call-start = ((), (), s32[]{:S(2)}) async-start(), calls=%async_computation.9 | async-start | bytes 131072 | tf_op jit(solution)/shard_map/psum | solution.py:52
  205.2 67.9 %all-reduce.15.cloned.1.call-start = ((), (), s32[]{:S(2)}) async-start(), calls=%async_computation.10 | async-start | bytes 131072 | tf_op jit(solution)/shard_map/psum | solution.py:52
  240.2 107.9 %all-reduce.17.cloned.1.call-start = ((), (), s32[]{:S(2)}) async-start(), calls=%async_computation.11 | async-start | bytes 131072 | tf_op jit(solution)/shard_map/psum | solution.py:52
  273.1 109.0 %all-reduce.19.cloned.1.call-start = ((), (), s32[]{:S(2)}) async-start(), calls=%async_computation.12 | async-start | bytes 131072 | tf_op jit(solution)/shard_map/psum | solution.py:52
  523.0 17.4 %all-to-all-start.7 = ((f32[16,96,128]{2,1,0:T(8,128)}), f32[16,96,128]{2,1,0:T(8,128)S(1)}, u32[]{:S(2)}, u32[]{:S(2)}) async-start(f32[16,96,128]{2,1,0:T(8,128)} %copy.23), calls=%async_computation.7 | async-start | bytes 1572864 | tf_op jit(solution)/shard_map/all_to_all | solution.py:46
  528.1 53.5 %all-reduce.21.cloned.1.call-start = ((), (), s32[]{:S(2)}) async-start(), calls=%async_computation.13 | async-start | bytes 131072 | tf_op jit(solution)/shard_map/psum | solution.py:52
  541.3 75.3 %all-reduce.23.cloned.1.call-start = ((), (), s32[]{:S(2)}) async-start(), calls=%async_computation.14 | async-start | bytes 131072 | tf_op jit(solution)/shard_map/psum | solution.py:52
  581.6 67.9 %all-reduce.25.cloned.1.call-start = ((), (), s32[]{:S(2)}) async-start(), calls=%async_computation.15 | async-start | bytes 131072 | tf_op jit(solution)/shard_map/psum | solution.py:52
  616.7 108.0 %all-reduce.27.cloned.1.call-start = ((), (), s32[]{:S(2)}) async-start(), calls=%async_computation.16 | async-start | bytes 131072 | tf_op jit(solution)/shard_map/psum | solution.py:52
  649.6 109.1 %all-reduce.29.cloned.1.call-start = ((), (), s32[]{:S(2)}) async-start(), calls=%async_computation.17 | async-start | bytes 131072 | tf_op jit(solution)/shard_map/psum | solution.py:52
Sparse Core Ops, SparseCore 0:
  164.4 40.6 all-reduce.10
  207.9 32.2 all-reduce.12
  242.9 30.1 all-reduce.14
  275.4 72.6 all-reduce.16
  350.4 31.5 all-reduce.18
  541.5 40.0 all-reduce.20
  584.3 32.2 all-reduce.22
  619.3 30.1 all-reduce.24
  652.0 72.6 all-reduce.26
  727.1 31.5 all-reduce.28
where the time goes:
time: 775 us; the launch traced here: 773 us
  waiting for transfers between devices  509 us (66%)
  blocking collectives  164 us (21%)
  matrix products  52.1 us (7%)
  starting transfers between devices  19.7 us (3%)
  between operations  15.6 us (2%)
    psum x10, waiting for transfers between devices, one_axis_at_a_time(): value = lax.psum(value, axis)  435 us
    all_to_all x3, blocking collectives, side_by_side(): lax.all_to_all(both, axis, split_axis=split_dim, concat_axis=concat_dim,...  146 us
    all_to_all x1, waiting for transfers between devices, side_by_side(): lax.all_to_all(both, axis, split_axis=split_dim, concat_axis=concat_dim,...  39.6 us
    all_to_all x2, waiting for transfers between devices, sum_at_owner(): lax.all_to_all(parts, axis, split_axis=0, concat_axis=0, tiled=True)  22.6 us
    dot_general x2, matrix products, on_device(): jnp.dot(hamiltonian_tiles, column_block, precision=lax.Precision.HIGHEST)  20.9 us
    all_to_all x1, blocking collectives, from_everyone(): lax.all_to_all(jnp.broadcast_to(value[None], (size, *value.shape)), axis,...  17.6 us
    dot_general x2, matrix products, on_device(): lax.dot_general(hamiltonian_tiles, row_block, (((0,), (0,)), ((), ())), p...  15.9 us
  transfers between devices with their start and end apart: 14, of which 14 were waited for; matrix products, arithmetic and copies ran while one was open for 0% of the time, Pallas kernels for 0%

commit v1 on v0

v1 whole, which is shorter than its diff:
```python
import jax
import jax.numpy as jnp
from jax import lax
from jax.experimental import pallas as pl
from jax.experimental.pallas import tpu as pltpu
from jax.sharding import PartitionSpec as P

NS_STEPS = 5
WIDE, NARROW = "wide", "narrow"
HIGH = lax.Precision.HIGH
HIGHEST = lax.Precision.HIGHEST


def exchange(parts, axis):
    return lax.all_to_all(parts, axis, 0, 0, tiled=True)


def to_everyone(value, axis):
    return exchange(jnp.broadcast_to(value[None], (lax.axis_size(axis), *value.shape)), axis)


def move_blocks(blocks, columns, scatter):
    count = blocks.shape[0]

    def kernel(columns_ref, blocks_ref, moved_ref):
        for i in range(count):
            column = columns_ref[i]
            if scatter:
                moved_ref[column] = blocks_ref[i]
            else:
                moved_ref[i] = blocks_ref[column]

    return pl.pallas_call(
        kernel,
        out_shape=jax.ShapeDtypeStruct(blocks.shape, blocks.dtype),
        in_specs=[
            pl.BlockSpec(memory_space=pltpu.SMEM),
            pl.BlockSpec(memory_space=pltpu.VMEM),
        ],
        out_specs=pl.BlockSpec(memory_space=pltpu.VMEM),
        cost_estimate=pl.CostEstimate(flops=0, bytes_accessed=8 * blocks.size, transcendentals=0),
    )(columns, blocks)


def apply_hamiltonian(tile, columns, vectors):
    rows, width = vectors.shape
    count = lax.axis_size(NARROW)
    with jax.named_scope("gather_wide"):
        slices = to_everyone(vectors, WIDE)
    with jax.named_scope("gather_row"):
        row_block = to_everyone(vectors, NARROW).reshape(count * rows, width)
    with jax.named_scope("gather_column"):
        picked = move_blocks(slices, columns, scatter=False)
        column_block = exchange(picked, NARROW).reshape(count * rows, width)
    with jax.named_scope("transposed"):
        transposed = lax.dot_general(tile, row_block, (((0,), (0,)), ((), ())), precision=HIGH)
    with jax.named_scope("direct"):
        direct = jnp.dot(tile, column_block, precision=HIGH)
    with jax.named_scope("back_transposed"):
        arrived = exchange(transposed.reshape(count, rows, width), NARROW)
        placed = move_blocks(arrived, columns, scatter=True)
    with jax.named_scope("back_direct"):
        direct_sum = exchange(direct.reshape(count, rows, width), NARROW).sum(axis=0)
    with jax.named_scope("back_wide"):
        transposed_sum = exchange(placed, WIDE).sum(axis=0)
    return direct_sum + transposed_sum


def sum_of_everyone(value):
    for axis in (WIDE, NARROW):
        size = lax.axis_size(axis)
        step = 1
        while step < size:
            value = value + lax.ppermute(value, axis, [(i, i ^ step) for i in range(size)])
            step *= 2
    return value


def inverse_root(gram, total_rows):
    identity = jnp.eye(gram.shape[0], dtype=jnp.float32)
    scale = jnp.sqrt(jnp.sum(gram * gram) + 1e-06)
    current = gram / scale
    inverse = identity
    for repeat in range(NS_STEPS):
        middle = 1.5 * identity - 0.5 * jnp.dot(inverse, current, precision=HIGHEST)
        current = jnp.dot(current, middle, precision=HIGHEST)
        inverse = jnp.dot(middle, inverse, precision=HIGHEST)
    return inverse * jnp.sqrt(total_rows / scale)


def gram_of(value):
    return lax.dot_general(value, value, (((0,), (0,)), ((), ())), precision=HIGHEST)


def on_device(tile, row_columns, start_vectors):
    total_rows = float(lax.axis_size(WIDE) * lax.axis_size(NARROW) * start_vectors.shape[0])
    columns = row_columns[0]
    first = apply_hamiltonian(tile, columns, start_vectors)
    second = apply_hamiltonian(tile, columns, first)
    with jax.named_scope("grams"):
        grams = sum_of_everyone(jnp.concatenate([gram_of(first), gram_of(second)], axis=0))
        gram_first, gram_second = jnp.split(grams, 2, axis=0)
    with jax.named_scope("inverse_first"):
        root_first = inverse_root(gram_first, total_rows)
    with jax.named_scope("inverse_second"):
        gram = jnp.dot(
            root_first.T, jnp.dot(gram_second, root_first, precision=HIGHEST), precision=HIGHEST
        )
        root_second = inverse_root(gram, total_rows)
    with jax.named_scope("finish"):
        return jnp.dot(
            jnp.dot(second, root_first, precision=HIGHEST), root_second, precision=HIGHEST
        )


def solution(mesh):
    return jax.shard_map(
        on_device,
        mesh=mesh,
        in_specs=(P(WIDE, NARROW), P(WIDE, None), P((WIDE, NARROW), None)),
        out_specs=P((WIDE, NARROW), None),
        check_vma=False,
    )
```

time: 775 us -> 365 us (0.47)
  waiting for transfers between devices: 509 us -> 198 us
  blocking collectives: 164 us -> 48 us
  starting transfers between devices: 19.7 us -> 51.3 us
  between operations: 15.6 us -> 2.02 us
  matrix products: 52.1 us -> 39 us
  local copies, waits for them, and re-layouts: 6.78 us -> 16 us
  Pallas kernels: 0 us -> 8.47 us
    psum x10 -> x0, waiting for transfers between devices: 435 us -> none  [one_axis_at_a_time(): value = lax.psum(value, axis)]
    all_to_all x4 -> x2, blocking collectives: 164 us -> 48 us  [exchange(): return lax.all_to_all(parts, axis, 0, 0, tiled=True)]
    all_to_all x4 -> x10, waiting for transfers between devices: 74.3 us -> 154 us  [exchange(): return lax.all_to_all(parts, axis, 0, 0, tiled=True)]
    ppermute x0 -> x8, waiting for transfers between devices: none -> 43.5 us  [sum_of_everyone(): lax.ppermute(value, axis, [(i, i ^ step) for i in range(size)])]
    all_to_all x4 -> x10, starting transfers between devices: 19.4 us -> 45.4 us  [exchange(): return lax.all_to_all(parts, axis, 0, 0, tiled=True)]
    dot_general x40 -> x38, matrix products: 52.1 us -> 39 us  [the longest x2 17.1 us: apply_hamiltonian(): direct = jnp.dot(tile, column_block, precision=HIGH)]
    unnamed x4 -> x7, local copies, waits for them, and re-layouts: 0.01 us -> 9.67 us
    pallas_call x0 -> x4, Pallas kernels: none -> 8.47 us  [move_blocks(): pl.pallas_call(kernel, out_shape=jax.ShapeDtypeStruct(blocks.shape, block...]
  transfers between devices with their start and end apart: 14 -> 18, of which waited for: 14 -> 18; matrix products, arithmetic and copies ran while one was open for 0% -> 12% of each run, Pallas kernels for 0% -> 2%
where the time goes in v1:
time: 365 us; the launch traced here: 363 us
  waiting for transfers between devices  198 us (54%)
  starting transfers between devices  51.3 us (14%)
  blocking collectives  48 us (13%)
  matrix products  39 us (11%)
  local copies, waits for them, and re-layouts  16 us (4%)
  Pallas kernels  8.47 us (2%)
    all_to_all x10, waiting for transfers between devices, exchange(): return lax.all_to_all(parts, axis, 0, 0, tiled=True)  154 us
    all_to_all x2, blocking collectives, exchange(): return lax.all_to_all(parts, axis, 0, 0, tiled=True)  48 us
    all_to_all x10, starting transfers between devices, exchange(): return lax.all_to_all(parts, axis, 0, 0, tiled=True)  45.4 us
    ppermute x8, waiting for transfers between devices, sum_of_everyone(): lax.ppermute(value, axis, [(i, i ^ step) for i in range(size)])  43.5 us
    dot_general x2, matrix products, apply_hamiltonian(): direct = jnp.dot(tile, column_block, precision=HIGH)  17.1 us
    dot_general x2, matrix products, apply_hamiltonian(): lax.dot_general(tile, row_block, (((0,), (0,)), ((), ())), precision=HIGH)  13.6 us
    unnamed x7, local copies, waits for them, and re-layouts  9.67 us
    pallas_call x4, Pallas kernels, move_blocks(): pl.pallas_call(kernel, out_shape=jax.ShapeDtypeStruct(blocks.shape, block...  8.47 us
  transfers between devices with their start and end apart: 18, of which 18 were waited for; matrix products, arithmetic and copies ran while one was open for 12% of the time, Pallas kernels for 2%

profile of v1, /device:TPU:8, one launch (start us, length us, event | category | flops | bytes accessed | tf_op | source)
XLA Modules:
  0.0 363.3 jit_solution(17658851230505470700)
XLA Ops:
  0.0 1.8 broadcast_in_dim.4
  1.8 18.4 %all_to_all.60.blocks_ref = f32[16,96,128]{2,1,0:T(8,128)} all-to-all(f32[16,96,128]{2,1,0:T(8,128)} %broadcast_in_dim.4), channel_id=1, replica_groups=mesh['wide'=16,'narrow'=16] {'wide'}, dimensions={0} | all-to-all | bytes 1572864 | tf_op jit(solution)/shard_map/gather_wide/all_to_all | solution.py:15
  20.2 9.8 %all-to-all-start.3 = ((f32[16,96,128]{2,1,0:T(8,128)}), f32[16,96,128]{2,1,0:T(8,128)S(1)}, u32[]{:S(2)}, u32[]{:S(2)}) async-start(f32[16,96,128]{2,1,0:T(8,128)} %broadcast_in_dim.4), calls=%async_computation.3 | async-start | bytes 1572864 | tf_op jit(solution)/shard_map/gather_row/all_to_all | solution.py:15
  30.1 2.1 gather_column.2
  32.2 23.2 %all-to-all-done.3 = f32[16,96,128]{2,1,0:T(8,128)S(1)} async-done(((f32[16,96,128]{2,1,0:T(8,128)}), f32[16,96,128]{2,1,0:T(8,128)S(1)}, u32[]{:S(2)}, u32[]{:S(2)}) %all-to-all-start.3) | async-done | bytes 786464 | tf_op jit(solution)/shard_map/gather_row/all_to_all | solution.py:15
  55.4 3.6 all-to-all-start.1
  59.0 9.7 %copy.7 = f32[1536,1536]{0,1:T(8,128)} copy(f32[1536,1536]{1,0:T(8,128)} %param.3) | data formatting | bytes 18874368 | tf_op args[0]
  68.6 7.2 %fusion.17 = f32[16,96,128]{2,1,0:T(8,128)} fusion(f32[16,96,1536]{2,1,0:T(8,128)} %bitcast.86, f32[1536,128,1]{1,0,2:T(8,128)S(1)} %bitcast.88), kind=kOutput, calls=%fused_computation.38 | convolution fusion | flops 1811939328 | bytes 11010048 | tf_op jit(solution)/shard_map/transposed/dot_general | solution.py:56
  75.9 6.2 %all-to-all-done.1 = f32[16,96,128]{2,1,0:T(8,128)S(1)} async-done(((f32[16,96,128]{2,1,0:T(8,128)}), f32[16,96,128]{2,1,0:T(8,128)S(1)}, u32[]{:S(2)}, u32[]{:S(2)}) %all-to-all-start.1) | async-done | bytes 786464 | tf_op jit(solution)/shard_map/gather_column/all_to_all | solution.py:15
  82.1 3.6 all-to-all-start.4
  85.7 8.6 %convolution_bitcast_fusion.2 = f32[1536,128]{0,1:T(8,128)S(1)} fusion(f32[1536,128]{1,0:T(8,128)S(1)} %bitcast.87, f32[1536,1536]{1,0:T(8,128)} %param.3), kind=kOutput, calls=%fused_computation.2 | convolution fusion | flops 1811939328 | bytes 11010048 | tf_op jit(solution)/shard_map/direct/dot_general | solution.py:58
  94.3 1.2 copy.6
  95.5 14.1 %all-to-all-done.4.blocks_ref = f32[16,96,128]{2,1,0:T(8,128)S(1)} async-done(((f32[16,96,128]{2,1,0:T(8,128)}), f32[16,96,128]{2,1,0:T(8,128)S(1)}, u32[]{:S(2)}, u32[]{:S(2)}) %all-to-all-start.4) | async-done | bytes 786464 | tf_op jit(solution)/shard_map/back_transposed/all_to_all | solution.py:15
  109.6 3.6 all-to-all-start.2
  113.2 2.1 back_transposed.2
  115.4 21.8 %all-to-all-done.2 = f32[16,96,128]{2,1,0:T(8,128)S(1)} async-done(((f32[16,96,128]{2,1,0:T(8,128)}), f32[16,96,128]{2,1,0:T(8,128)S(1)}, u32[]{:S(2)}, u32[]{:S(2)}) %all-to-all-start.2) | async-done | bytes 786464 | tf_op jit(solution)/shard_map/back_direct/all_to_all | solution.py:15
  137.2 5.1 %all-to-all-start.5 = ((f32[16,96,128]{2,1,0:T(8,128)}), f32[16,96,128]{2,1,0:T(8,128)S(1)}, u32[]{:S(2)}, u32[]{:S(2)}) async-start(f32[16,96,128]{2,1,0:T(8,128)} %back_transposed.2), calls=%async_computation.5 | async-start | bytes 1572864 | tf_op jit(solution)/shard_map/back_wide/all_to_all | solution.py:15
  142.3 12.2 %all-to-all-done.5 = f32[16,96,128]{2,1,0:T(8,128)S(1)} async-done(((f32[16,96,128]{2,1,0:T(8,128)}), f32[16,96,128]{2,1,0:T(8,128)S(1)}, u32[]{:S(2)}, u32[]{:S(2)}) %all-to-all-start.5) | async-done | bytes 786464 | tf_op jit(solution)/shard_map/back_wide/all_to_all | solution.py:15
  154.6 1.0 broadcast_in_dim.5
  155.5 29.5 %all_to_all.61 = f32[16,96,128]{2,1,0:T(8,128)S(1)} all-to-all(f32[16,96,128]{2,1,0:T(8,128)} %broadcast_in_dim.5), channel_id=1, replica_groups=mesh['wide'=16,'narrow'=16] {'narrow'}, dimensions={0} | all-to-all | bytes 1572864 | tf_op jit(solution)/shard_map/gather_row/all_to_all | solution.py:15
  185.1 4.3 %all-to-all-start.6 = ((f32[16,96,128]{2,1,0:T(8,128)}), f32[16,96,128]{2,1,0:T(8,128)S(1)}, u32[]{:S(2)}, u32[]{:S(2)}) async-start(f32[16,96,128]{2,1,0:T(8,128)} %broadcast_in_dim.5), calls=%async_computation.6 | async-start | bytes 1572864 | tf_op jit(solution)/shard_map/gather_wide/all_to_all | solution.py:15
  189.3 6.4 %convolution_bitcast_fusion = f32[1536,128]{0,1:T(8,128)S(1)} fusion(f32[1536,128]{1,0:T(8,128)S(1)} %bitcast.90, f32[1536,1536]{1,0:T(8,128)} %param.3), kind=kOutput, calls=%fused_computation | convolution fusion | flops 1811939328 | bytes 11010048 | tf_op jit(solution)/shard_map/transposed/dot_general | solution.py:56
  195.7 1.2 copy.9
  196.9 4.6 %all-to-all-done.6.blocks_ref = f32[16,96,128]{2,1,0:T(8,128)S(1)} async-done(((f32[16,96,128]{2,1,0:T(8,128)}), f32[16,96,128]{2,1,0:T(8,128)S(1)}, u32[]{:S(2)}, u32[]{:S(2)}) %all-to-all-start.6) | async-done | bytes 786464 | tf_op jit(solution)/shard_map/gather_wide/all_to_all | solution.py:15
  201.5 3.8 %all-to-all-start.10 = ((f32[16,96,128]{2,1,0:T(8,128)}), f32[16,96,128]{2,1,0:T(8,128)S(1)}, u32[]{:S(2)}, u32[]{:S(2)}) async-start(f32[16,96,128]{2,1,0:T(8,128)} %bitcast.13), calls=%async_computation.10 | async-start | bytes 1572864 | tf_op jit(solution)/shard_map/back_transposed/all_to_all | solution.py:15
  205.3 2.1 gather_column.3
  207.4 23.4 %all-to-all-done.10.blocks_ref = f32[16,96,128]{2,1,0:T(8,128)S(1)} async-done(((f32[16,96,128]{2,1,0:T(8,128)}), f32[16,96,128]{2,1,0:T(8,128)S(1)}, u32[]{:S(2)}, u32[]{:S(2)}) %all-to-all-start.10) | async-done | bytes 786464 | tf_op jit(solution)/shard_map/back_transposed/all_to_all | solution.py:15
  230.9 3.6 all-to-all-start.7
  234.5 2.1 back_transposed.3
  236.7 20.9 %all-to-all-done.7 = f32[16,96,128]{2,1,0:T(8,128)S(1)} async-done(((f32[16,96,128]{2,1,0:T(8,128)}), f32[16,96,128]{2,1,0:T(8,128)S(1)}, u32[]{:S(2)}, u32[]{:S(2)}) %all-to-all-start.7) | async-done | bytes 786464 | tf_op jit(solution)/shard_map/gather_column/all_to_all | solution.py:15
  257.6 4.3 %all-to-all-start.11 = ((f32[16,96,128]{2,1,0:T(8,128)}), f32[16,96,128]{2,1,0:T(8,128)S(1)}, u32[]{:S(2)}, u32[]{:S(2)}) async-start(f32[16,96,128]{2,1,0:T(8,128)} %back_transposed.3), calls=%async_computation.11 | async-start | bytes 1572864 | tf_op jit(solution)/shard_map/back_wide/all_to_all | solution.py:15
  261.9 8.5 %convolution_bitcast_fusion.1 = f32[1536,128]{0,1:T(8,128)S(1)} fusion(f32[1536,128]{1,0:T(8,128)S(1)} %bitcast.89, f32[1536,1536]{1,0:T(8,128)} %param.3), kind=kOutput, calls=%fused_computation.1 | convolution fusion | flops 1811939328 | bytes 11010048 | tf_op jit(solution)/shard_map/direct/dot_general | solution.py:58
  270.4 1.2 copy.8
  271.6 2.4 all-to-all-done.11
  274.1 3.6 all-to-all-start.8
  278.0 25.2 %all-to-all-done.8 = f32[16,96,128]{2,1,0:T(8,128)S(1)} async-done(((f32[16,96,128]{2,1,0:T(8,128)}), f32[16,96,128]{2,1,0:T(8,128)S(1)}, u32[]{:S(2)}, u32[]{:S(2)}) %all-to-all-start.8) | async-done | bytes 786464 | tf_op jit(solution)/shard_map/back_direct/all_to_all | solution.py:15
  303.7 1.3 collective-permute-done
  305.3 5.4 %collective-permute-done.1 = f32[256,128]{1,0:T(8,128)S(1)} collective-permute-done((f32[256,128]{1,0:T(8,128)S(1)}, f32[256,128]{1,0:T(8,128)S(1)}, u32[]{:S(2)}, u32[]{:S(2)}) %collective-permute-start.1) | collective-permute-done | bytes 131104 | tf_op jit(solution)/shard_map/grams/ppermute | solution.py:74
  310.8 5.0 %collective-permute-done.2 = f32[256,128]{1,0:T(8,128)S(1)} collective-permute-done((f32[256,128]{1,0:T(8,128)S(1)}, f32[256,128]{1,0:T(8,128)S(1)}, u32[]{:S(2)}, u32[]{:S(2)}) %collective-permute-start.2) | collective-permute-done | bytes 131104 | tf_op jit(solution)/shard_map/grams/ppermute | solution.py:74
  315.8 1.7 collective-permute-start.3
  317.5 4.9 %collective-permute-done.3 = f32[256,128]{1,0:T(8,128)S(1)} collective-permute-done((f32[256,128]{1,0:T(8,128)S(1)}, f32[256,128]{1,0:T(8,128)S(1)}, u32[]{:S(2)}, u32[]{:S(2)}) %collective-permute-start.3) | collective-permute-done | bytes 131104 | tf_op jit(solution)/shard_map/grams/ppermute | solution.py:74
  323.0 5.9 %collective-permute-done.4 = f32[256,128]{1,0:T(8,128)S(1)} collective-permute-done((f32[256,128]{1,0:T(8,128)S(1)}, f32[256,128]{1,0:T(8,128)S(1)}, u32[]{:S(2)}, u32[]{:S(2)}) %collective-permute-start.4) | collective-permute-done | bytes 131104 | tf_op jit(solution)/shard_map/grams/ppermute | solution.py:74
  329.1 6.4 %collective-permute-done.5 = f32[256,128]{1,0:T(8,128)S(1)} collective-permute-done((f32[256,128]{1,0:T(8,128)S(1)}, f32[256,128]{1,0:T(8,128)S(1)}, u32[]{:S(2)}, u32[]{:S(2)}) %collective-permute-start.5) | collective-permute-done | bytes 131104 | tf_op jit(solution)/shard_map/grams/ppermute | solution.py:74
  335.5 7.7 %collective-permute-done.6 = f32[256,128]{1,0:T(8,128)S(1)} collective-permute-done((f32[256,128]{1,0:T(8,128)S(1)}, f32[256,128]{1,0:T(8,128)S(1)}, u32[]{:S(2)}, u32[]{:S(2)}) %collective-permute-start.6) | collective-permute-done | bytes 131104 | tf_op jit(solution)/shard_map/grams/ppermute | solution.py:74
  343.2 2.9 collective-permute-start.7
  346.2 6.9 %collective-permute-done.7 = f32[256,128]{1,0:T(8,128)S(1)} collective-permute-done((f32[256,128]{1,0:T(8,128)S(1)}, f32[256,128]{1,0:T(8,128)S(1)}, u32[]{:S(2)}, u32[]{:S(2)}) %collective-permute-start.7) | collective-permute-done | bytes 131104 | tf_op jit(solution)/shard_map/grams/ppermute | solution.py:74
  357.9 0.9 multiply_reduce_fusion
  362.5 0.8 fusion.33
  (60 shorter events, 8.8 us)
Async XLA Ops:
  20.2 35.1 %all-to-all-start.3 = ((f32[16,96,128]{2,1,0:T(8,128)}), f32[16,96,128]{2,1,0:T(8,128)S(1)}, u32[]{:S(2)}, u32[]{:S(2)}) async-start(f32[16,96,128]{2,1,0:T(8,128)} %broadcast_in_dim.4), calls=%async_computation.3 | async-start | bytes 1572864 | tf_op jit(solution)/shard_map/gather_row/all_to_all | solution.py:15
  55.4 26.7 %all-to-all-start.1 = ((f32[16,96,128]{2,1,0:T(8,128)}), f32[16,96,128]{2,1,0:T(8,128)S(1)}, u32[]{:S(2)}, u32[]{:S(2)}) async-start(f32[16,96,128]{2,1,0:T(8,128)} %gather_column.2), calls=%async_computation.1 | async-start | bytes 1572864 | tf_op jit(solution)/shard_map/gather_column/all_to_all | solution.py:15
  82.1 27.5 %all-to-all-start.4 = ((f32[16,96,128]{2,1,0:T(8,128)}), f32[16,96,128]{2,1,0:T(8,128)S(1)}, u32[]{:S(2)}, u32[]{:S(2)}) async-start(f32[16,96,128]{2,1,0:T(8,128)} %fusion.17), calls=%async_computation.4 | async-start | bytes 1572864 | tf_op jit(solution)/shard_map/back_transposed/all_to_all | solution.py:15
  109.6 3.6 copy-start
  109.6 27.6 %all-to-all-start.2 = ((f32[16,96,128]{2,1,0:T(8,128)}), f32[16,96,128]{2,1,0:T(8,128)S(1)}, u32[]{:S(2)}, u32[]{:S(2)}) async-start(f32[16,96,128]{2,1,0:T(8,128)} %bitcast.3), calls=%async_computation.2 | async-start | bytes 1572864 | tf_op jit(solution)/shard_map/back_direct/all_to_all | solution.py:15
  137.2 17.3 %all-to-all-start.5 = ((f32[16,96,128]{2,1,0:T(8,128)}), f32[16,96,128]{2,1,0:T(8,128)S(1)}, u32[]{:S(2)}, u32[]{:S(2)}) async-start(f32[16,96,128]{2,1,0:T(8,128)} %back_transposed.2), calls=%async_computation.5 | async-start | bytes 1572864 | tf_op jit(solution)/shard_map/back_wide/all_to_all | solution.py:15
  185.1 16.5 %all-to-all-start.6 = ((f32[16,96,128]{2,1,0:T(8,128)}), f32[16,96,128]{2,1,0:T(8,128)S(1)}, u32[]{:S(2)}, u32[]{:S(2)}) async-start(f32[16,96,128]{2,1,0:T(8,128)} %broadcast_in_dim.5), calls=%async_computation.6 | async-start | bytes 1572864 | tf_op jit(solution)/shard_map/gather_wide/all_to_all | solution.py:15
  201.5 3.8 %copy-start.1 = (f32[16,96,128]{2,1,0:T(8,128)}, f32[16,96,128]{2,1,0:T(8,128)S(1)}, u32[]{:S(2)}) copy-start(f32[16,96,128]{2,1,0:T(8,128)S(1)} %all-to-all-done.6.blocks_ref) | copy-start | bytes 2359300
  201.5 29.4 %all-to-all-start.10 = ((f32[16,96,128]{2,1,0:T(8,128)}), f32[16,96,128]{2,1,0:T(8,128)S(1)}, u32[]{:S(2)}, u32[]{:S(2)}) async-start(f32[16,96,128]{2,1,0:T(8,128)} %bitcast.13), calls=%async_computation.10 | async-start | bytes 1572864 | tf_op jit(solution)/shard_map/back_transposed/all_to_all | solution.py:15
  230.9 3.6 copy-start.2
  230.9 26.7 %all-to-all-start.7 = ((f32[16,96,128]{2,1,0:T(8,128)}), f32[16,96,128]{2,1,0:T(8,128)S(1)}, u32[]{:S(2)}, u32[]{:S(2)}) async-start(f32[16,96,128]{2,1,0:T(8,128)} %gather_column.3), calls=%async_computation.7 | async-start | bytes 1572864 | tf_op jit(solution)/shard_map/gather_column/all_to_all | solution.py:15
  257.6 16.5 %all-to-all-start.11 = ((f32[16,96,128]{2,1,0:T(8,128)}), f32[16,96,128]{2,1,0:T(8,128)S(1)}, u32[]{:S(2)}, u32[]{:S(2)}) async-start(f32[16,96,128]{2,1,0:T(8,128)} %back_transposed.3), calls=%async_computation.11 | async-start | bytes 1572864 | tf_op jit(solution)/shard_map/back_wide/all_to_all | solution.py:15
  274.1 29.2 %all-to-all-start.8 = ((f32[16,96,128]{2,1,0:T(8,128)}), f32[16,96,128]{2,1,0:T(8,128)S(1)}, u32[]{:S(2)}, u32[]{:S(2)}) async-start(f32[16,96,128]{2,1,0:T(8,128)} %bitcast.10), calls=%async_computation.8 | async-start | bytes 1572864 | tf_op jit(solution)/shard_map/back_direct/all_to_all | solution.py:15
  303.6 1.4 collective-permute-start
  305.1 5.6 %collective-permute-start.1 = (f32[256,128]{1,0:T(8,128)S(1)}, f32[256,128]{1,0:T(8,128)S(1)}, u32[]{:S(2)}, u32[]{:S(2)}) collective-permute-start(f32[256,128]{1,0:T(8,128)S(1)} %fusion.16), channel_id=1, source_target_pairs={{0,32},{16,48},{32,0},{48,16},{64,96},{80,112},{96,64},{112,80},{1... | collective-permute-start | bytes 393224 | tf_op jit(solution)/shard_map/grams/ppermute | solution.py:74
  310.7 5.1 %collective-permute-start.2 = (f32[256,128]{1,0:T(8,128)S(1)}, f32[256,128]{1,0:T(8,128)S(1)}, u32[]{:S(2)}, u32[]{:S(2)}) collective-permute-start(f32[256,128]{1,0:T(8,128)S(1)} %add.43), channel_id=1, source_target_pairs={{0,64},{16,80},{32,96},{48,112},{64,0},{80,16},{96,32},{112,48},{1... | collective-permute-start | bytes 393224 | tf_op jit(solution)/shard_map/grams/ppermute | solution.py:74
  315.8 6.6 %collective-permute-start.3 = (f32[256,128]{1,0:T(8,128)S(1)}, f32[256,128]{1,0:T(8,128)S(1)}, u32[]{:S(2)}, u32[]{:S(2)}) collective-permute-start(f32[256,128]{1,0:T(8,128)S(1)} %add.44), channel_id=1, source_target_pairs={{0,128},{16,144},{32,160},{48,176},{64,192},{80,208},{96,224},{112... | collective-permute-start | bytes 393224 | tf_op jit(solution)/shard_map/grams/ppermute | solution.py:74
  322.4 6.6 %collective-permute-start.4 = (f32[256,128]{1,0:T(8,128)S(1)}, f32[256,128]{1,0:T(8,128)S(1)}, u32[]{:S(2)}, u32[]{:S(2)}) collective-permute-start(f32[256,128]{1,0:T(8,128)S(1)} %add.45), channel_id=1, source_target_pairs={{0,1},{1,0},{2,3},{3,2},{4,5},{5,4},{6,7},{7,6},{8,9},{9,8},{10,11... | collective-permute-start | bytes 393224 | tf_op jit(solution)/shard_map/grams/ppermute | solution.py:74
  329.0 6.5 %collective-permute-start.5 = (f32[256,128]{1,0:T(8,128)S(1)}, f32[256,128]{1,0:T(8,128)S(1)}, u32[]{:S(2)}, u32[]{:S(2)}) collective-permute-start(f32[256,128]{1,0:T(8,128)S(1)} %add.46), channel_id=1, source_target_pairs={{0,2},{1,3},{2,0},{3,1},{4,6},{5,7},{6,4},{7,5},{8,10},{9,11},{10,... | collective-permute-start | bytes 393224 | tf_op jit(solution)/shard_map/grams/ppermute | solution.py:74
  335.4 7.8 %collective-permute-start.6 = (f32[256,128]{1,0:T(8,128)S(1)}, f32[256,128]{1,0:T(8,128)S(1)}, u32[]{:S(2)}, u32[]{:S(2)}) collective-permute-start(f32[256,128]{1,0:T(8,128)S(1)} %add.47), channel_id=1, source_target_pairs={{0,4},{1,5},{2,6},{3,7},{4,0},{5,1},{6,2},{7,3},{8,12},{9,13},{10,... | collective-permute-start | bytes 393224 | tf_op jit(solution)/shard_map/grams/ppermute | solution.py:74
  343.2 9.9 %collective-permute-start.7 = (f32[256,128]{1,0:T(8,128)S(1)}, f32[256,128]{1,0:T(8,128)S(1)}, u32[]{:S(2)}, u32[]{:S(2)}) collective-permute-start(f32[256,128]{1,0:T(8,128)S(1)} %add.48), channel_id=1, source_target_pairs={{0,8},{1,9},{2,10},{3,11},{4,12},{5,13},{6,14},{7,15},{8,0},{9,1},... | collective-permute-start | bytes 393224 | tf_op jit(solution)/shard_map/grams/ppermute | solution.py:74
